TPU v7x, 256 devices: a whole 4x4x8 slice. The times are simulated.
256 devices in a mesh: dom: 4 (over x), dp: 64 (over z, y, core).
Axes of the slice: x: 4, y: 4, z: 8, core: 2. Of those that a mesh axis runs over, the one named last changes fastest.
Arguments:
- records: bfloat16 [131072, 2048], P('dp'), may hold values from -6 to 6
- counts_obs: int32 [131072], P('dp'), may hold values from 0 to 7
- exposure_bin: int32 [131072], P('dp'), may hold values from 0 to 63
- bin_offset: float32 [64], replicated, may hold values from -1.5 to 0.5
- theta: float32 [2048, 2048], P('dom', 'dp'), may hold values from -6 to 6
- noise: float32 [2048, 2048], P('dom', 'dp'), may hold values from -6 to 6
- offspring: int32 [2048], replicated, may hold values from 0 to 16, as said below
- slot_order: int32 [2048], replicated, may hold values from 0 to 2047, each once
- temper_step: float32 [], replicated, may hold values from 0.0069053397 to 0.013810679
- temper_level: float32 [], replicated, may hold values from 0.5 to 2
- step_size: float32 [], replicated, may hold values from 0.02 to 0.1
Outputs:
- moved: float32 [2048, 2048], P('dom', 'dp')
- log_evidence: float32 [], replicated
- ess_fraction: float32 [], replicated
Inputs may be any that keep to these rules, and one draw needn't show every extreme that they name: The counts sum to 2048: 32 particles have 16 offspring, half of the particles one, an eighth two, the rest none, placed in random order. `slot_order`: each slot appears once.
All inputs are finite; a program needn't handle non-finite values.
Results may differ from a plain program's by a relative error of at most 0.0028.
The roundings to bfloat16 on the way count: a program that leaves them out, or rounds other values in their place, can miss the bound.
Values may be sent and summed in bfloat16 or wider, within the bound.
A program may use at most 64 MiB of HBM per device.

v0:
```python
import math

import jax
import jax.numpy as jnp
from jax import lax
from jax.sharding import PartitionSpec as P


def on_device(
    records,
    counts_obs,
    exposure_bin,
    bin_offset,
    theta,
    noise,
    offspring,
    slot_order,
    temper_step,
    temper_level,
    step_size,
):
    row_count, feature_count = records.shape
    part_count, col_count = theta.shape
    group_count = lax.axis_size("dom")
    shard_count = lax.axis_size("dp")
    scale_in = 1.0 / math.sqrt(feature_count)
    temper_scale = math.sqrt(feature_count / (row_count * shard_count))
    bin_ids = jnp.arange(bin_offset.shape[0], dtype=jnp.int32)
    one_hot = exposure_bin[:, None] == bin_ids[None, :]
    offset = jnp.sum(jnp.where(one_hot, bin_offset[None, :], 0.0), axis=1)
    theta_low = theta.astype(jnp.bfloat16)
    gathered = lax.all_gather(theta_low, "dp", axis=1, tiled=True)
    products = lax.dot_general(
        records, gathered, (((1,), (1,)), ((), ())), preferred_element_type=jnp.float32
    )
    linear = products * scale_in + offset[:, None]
    intensity = jnp.exp(linear)
    target = counts_obs.astype(jnp.float32)
    factorial_total = jnp.sum(jax.scipy.special.gammaln(target + 1.0))
    local_loglik = jnp.sum(target[:, None] * linear - intensity, axis=0) - factorial_total
    residual = (target[:, None] - intensity).astype(jnp.bfloat16)
    score_cols = lax.psum_scatter(
        lax.dot_general(
            records, residual, (((0,), (0,)), ((), ())), preferred_element_type=jnp.float32
        ),
        "dp",
        scatter_dimension=0,
        tiled=True,
    )
    loglik = lax.psum(local_loglik, "dp")
    log_weight = temper_step * temper_scale * loglik
    peak_value = lax.pmax(jnp.max(log_weight), "dom")
    shifted = jnp.exp(log_weight - peak_value)
    weight_sum, weight_square = lax.psum((jnp.sum(shifted), jnp.sum(shifted * shifted)), "dom")
    particle_total = part_count * group_count
    log_evidence = peak_value + jnp.log(weight_sum) - math.log(particle_total)
    ess_fraction = weight_sum * weight_sum / (weight_square * particle_total)
    drift_term = -theta + temper_level * (temper_scale * scale_in) * score_cols.T
    everyone, parent_drift = (
        lax.all_gather(theta, "dom", axis=0, tiled=True),
        lax.all_gather(drift_term, "dom", axis=0, tiled=True),
    )
    cumulative = jnp.cumsum(offspring)
    first_slot = lax.axis_index("dom") * part_count
    slot_index = lax.dynamic_slice_in_dim(slot_order, first_slot, part_count, 0)
    parent = jnp.sum((cumulative[None, :] <= slot_index[:, None]).astype(jnp.int32), axis=1)
    moved_theta = (
        jnp.take(everyone, parent, axis=0)
        + 0.5 * step_size * jnp.take(parent_drift, parent, axis=0)
        + jnp.sqrt(step_size) * noise
    )
    return (moved_theta, log_evidence, ess_fraction)


def solution(mesh):
    in_specs = (
        P("dp", None),
        P("dp"),
        P("dp"),
        P(),
        P("dom", "dp"),
        P("dom", "dp"),
        P(),
        P(),
        P(),
        P(),
        P(),
    )
    out_specs = (P("dom", "dp"), P(), P())
    return jax.shard_map(
        on_device, mesh=mesh, in_specs=in_specs, out_specs=out_specs, check_vma=False
    )
```

profile of v0, /device:TPU:2, one launch (start us, length us, event | category | flops | bytes accessed | tf_op | source)
XLA Modules:
  0.0 308.2 jit_solution(12798264481511224179)
XLA Ops:
  7.2 1.5 convert_element_type.14
  8.7 0.0 reduce-scatter.4.cloned.1.call-start
  8.7 0.7 convert_element_type.13
  9.4 0.9 select_reduce_fusion
  10.3 81.3 %all-gather.2.cloned.1.call-done = bf16[512,2048]{0,1:T(8,128)(2,1)} async-done(((bf16[512,32]{0,1:T(8,128)(2,1)}), bf16[512,2048]{0,1:T(8,128)(2,1)}) %all-gather.2.cloned.1.call-update) | async-done | bytes 2097168 | tf_op jit(solution)/shard_map/all_gather | solution.py:32
  91.6 8.2 %subtract_reduce_fusion = (f32[512]{0:T(512)S(1)}, f32[2048,512]{1,0:T(8,128)S(1)}) fusion(f32[2048]{0:T(1024)S(1)} %select_reduce_fusion, f32[2048]{0:T(1024)S(1)} %convert_element_type.13, bf16[2048,2048]{1,0:T(8,128)(2,1)} %param.13, bf16[512,2048]{0,1:T(8,128)(2,1)} %all-gather.2.cloned.1.call-done), kind=kOutput, calls=%fused_computation.2 | convolution fusion | flops 4300209664 | bytes 14698496 | tf_op jit(solution)/shard_map/dot_general | solution.py:33
  99.8 7.1 %convolution_bitcast_fusion = f32[2048,512]{0,1:T(8,128)} fusion(bf16[2048,2048]{1,0:T(8,128)(2,1)S(1)} %copy-done.4, f32[2048,512]{1,0:T(8,128)S(1)} %get-tuple-element.24, f32[2048]{0:T(1024)S(1)} %select_reduce_fusion, f32[2048]{0:T(1024)S(1)} %convert_element_type.13), kind=kOutput, calls=%fused_computation.6 | convolution fusion | flops 4299161600 | bytes 16793600 | tf_op jit(solution)/shard_map/dot_general | solution.py:43
  107.0 5.3 %copy.35 = f32[2048,512]{1,0:T(8,128)} copy(f32[2048,512]{0,1:T(8,128)} %convolution_bitcast_fusion) | data formatting | bytes 8388608
  112.3 0.8 copy-done
  113.1 0.1 copy.30
  113.9 0.3 reduce-window.9
  114.2 0.1 slice.13
  114.3 0.1 copy.33
  115.8 0.8 dynamic_slice.3
  116.6 15.5 %all_gather.9 = f32[2048,32]{1,0:T(8,128)S(1)} all-gather(f32[512,32]{1,0:T(8,128)S(1)} %copy.30), channel_id=1, replica_groups=mesh['dom'=4,'dp'=64] {'dom'}, dimensions={0}, use_global_device_ids=true | all-gather | bytes 327680 | tf_op jit(solution)/shard_map/all_gather | solution.py:60
  132.1 0.1 slice_reduce_fusion
  132.2 0.1 add_bitcast_fusion
  132.3 0.6 convert_reduce_fusion
  132.9 0.7 select_reduce_fusion.1
  133.6 0.6 broadcast_subtract_fusion
  134.2 124.4 %psum.21 = f32[512]{0:T(512)S(1)} all-reduce(f32[512]{0:T(512)S(1)} %broadcast_subtract_fusion), channel_id=1, replica_groups=mesh['dom'=4,'dp'=64] {'dp'}, use_global_device_ids=true, to_apply=%region_7.0 | all-reduce | flops 512 | bytes 4096 | tf_op jit(solution)/shard_map/psum | solution.py:50
  258.6 0.6 multiply_reduce_fusion.1
  259.2 1.0 gather_fusion
  260.2 9.0 %pmax.7 = f32[]{:T(128)} all-reduce(f32[]{:T(128)} %multiply_reduce_fusion.1), channel_id=1, replica_groups=mesh['dom'=4,'dp'=64] {'dom'}, use_global_device_ids=true, to_apply=%region_9.0 | all-reduce | flops 1 | bytes 8 | tf_op jit(solution)/shard_map/pmax | solution.py:52
  269.2 1.3 multiply_reduce_fusion
  270.4 11.0 %all-reduce = (f32[]{:T(128)}, f32[]{:T(128)}) all-reduce(f32[]{:T(128)} %get-tuple-element.20, f32[]{:T(128)} %get-tuple-element.19), channel_id=1, replica_groups=mesh['dom'=4,'dp'=64] {'dom'}, use_global_device_ids=true, to_apply=%region_11.0 | all-reduce | flops 2 | bytes 16 | tf_op jit(solution)/shard_map/psum | solution.py:54
  284.7 0.9 bitcast_add_fusion
  285.6 11.2 %all_gather.11 = f32[2048,32]{0,1:T(8,128)S(1)} all-gather(f32[512,32]{0,1:T(8,128)S(1)} %bitcast_add_fusion), channel_id=1, replica_groups=mesh['dom'=4,'dp'=64] {'dom'}, dimensions={0}, use_global_device_ids=true | all-gather | bytes 327680 | tf_op jit(solution)/shard_map/all_gather | solution.py:61
  296.8 0.3 copy.32
  297.1 1.0 gather_fusion.1
  298.2 0.1 fusion.4
  298.3 0.7 copy.34
  (17 shorter events, 0.2 us)
Async XLA Ops:
  7.2 84.4 %all-gather.2.cloned.1.call-start = ((), (), s32[]{:S(2)}) async-start(), calls=%async_computation.1 | async-start | bytes 2129920 | tf_op jit(solution)/shard_map/all_gather | solution.py:32
  8.7 276.0 %reduce-scatter.4.cloned.1.call-start = ((), (), s32[]{:S(2)}) async-start(), calls=%async_computation.2 | async-start | bytes 4259840 | tf_op jit(solution)/shard_map/reduce_scatter | solution.py:42
  91.6 8.2 %copy-start.4 = (bf16[2048,2048]{1,0:T(8,128)(2,1)S(1)}, bf16[2048,2048]{1,0:T(8,128)(2,1)}, u32[]{:S(2)}) copy-start(bf16[2048,2048]{1,0:T(8,128)(2,1)} %param.13) | copy-start | bytes 25165828
  112.3 0.8 copy-start
  112.3 1.6 copy-start.2
  112.3 2.0 copy-start.1
  112.3 20.6 %copy-start.3 = (s32[2048]{0:T(1024)S(1)}, s32[2048]{0:T(1024)}, u32[]{:S(2)}) copy-start(s32[2048]{0:T(1024)} %param.14) | copy-start | bytes 24580
Sparse Core Ops, SparseCore 0:
  11.3 80.2 all-gather.1
  112.5 141.6 reduce-scatter.3
where the time goes:
time: 309 us; the launch traced here: 308 us
  blocking collectives  171 us (55%)
  waiting for transfers between devices  81.3 us (26%)
  between operations  21.7 us (7%)
  matrix products  15.3 us (5%)
  local copies, waits for them, and re-layouts  10.5 us (3%)
  other arithmetic  8.22 us (3%)
    psum x1, blocking collectives, on_device(): loglik = lax.psum(local_loglik, 'dp')  124 us
    all_gather x1, waiting for transfers between devices, on_device(): gathered = lax.all_gather(theta_low, 'dp', axis=1, tiled=True)  81.3 us
    all_gather x1, blocking collectives, on_device(): lax.all_gather(theta, 'dom', axis=0, tiled=True)  15.5 us
    all_gather x1, blocking collectives, on_device(): lax.all_gather(drift_term, 'dom', axis=0, tiled=True)  11.2 us
    psum x1, blocking collectives, on_device(): lax.psum((jnp.sum(shifted), jnp.sum(shifted * shifted)), 'dom')  11 us
    pmax x1, blocking collectives, on_device(): peak_value = lax.pmax(jnp.max(log_weight), 'dom')  8.96 us
    dot_general x1, matrix products, on_device(): lax.dot_general(records, gathered, (((1,), (1,)), ((), ())), preferred_el...  8.2 us
    unnamed x14, local copies, waits for them, and re-layouts  7.14 us
  transfers between devices with their start and end apart: 2, of which 1 were waited for; matrix products, arithmetic and copies ran while one was open for 3% of the time, Pallas kernels for 0%

commit v1 on v0

v1 whole, which is shorter than its diff:
```python
import functools
import math

import jax
import jax.numpy as jnp
from jax import lax
from jax.experimental import pallas as pl
from jax.experimental.pallas import tpu as pltpu
from jax.sharding import PartitionSpec as P

F32, BF16 = jnp.float32, jnp.bfloat16
MESH = pl.DeviceIdType.MESH
NZ, NY, NX = 8, 4, 4
Z_ORDER = (4, 3, 5, 2, 6, 1, 7)
Z_ARRIVE = (1, 7, 2, 6, 3, 5, 4)
Y_STEPS = (2, 1, 3, 0)


def kernel(
    rec_hbm, cnt_ref, bin_ref, bo_ref, th_ref, nz_ref, offs_ref, slot_ref, tstep_ref, tlev_ref, step_ref,
    out_ref, le_ref, ess_ref,
    rec, rect, thg, res, offb, cntb, sel, thx, base, scf, snd_c, rcv_c, snd_y, rcv_y, snd_z, rcv_z, scx,
    ll_own, ll_c, ll_y, ll_z, ll_x,
    rec_sem, gz_s, gz_r, gy_s, gy_r, gc_s, gc_r, tx_s, tx_r, c_s, c_r, y_s, y_r, z_s, z_r, x_s, x_r,
    lc_s, lc_r, ly_s, ly_r, lz_s, lz_r, lx_s, lx_r,
):
    x = lax.axis_index("dom")
    dp = lax.axis_index("dp")
    z, y, c = dp // 8, (dp // 2) % 4, dp % 2
    n_rec, n_feat = rec.shape
    n_part = th_ref.shape[1]
    scale_in = 1.0 / math.sqrt(n_feat)
    temper_scale = math.sqrt(n_feat / (n_rec * NZ * NY * 2))

    def at(zz, yy, cc):
        return (x, zz * 8 + yy * 2 + cc)

    sib = at(z, y, 1 - c)
    zs = [lax.rem(z + k, NZ) for k in range(NZ)]
    ys = [lax.rem(y + k, NY) for k in range(NY)]
    xs = [lax.rem(x + k, NX) for k in range(NX)]

    barrier = pltpu.get_barrier_semaphore()
    peers = [sib] + [at(zs[k], y, c) for k in Z_ORDER] + [at(z, ys[k], c) for k in (2, 1, 3)] + [(xs[k], dp) for k in (2, 1, 3)]
    for peer in peers:
        pl.semaphore_signal(barrier, inc=1, device_id=peer, device_id_type=MESH)

    blk = n_rec // 8
    loads = []
    for i in range(8):
        cp = pltpu.make_async_copy(rec_hbm.at[pl.ds(i * blk, blk)], rec.at[pl.ds(i * blk, blk)], rec_sem.at[i])
        cp.start()
        loads.append(cp)

    theta = th_ref[...]
    thg[z, y, c] = theta.astype(BF16)
    thx[x] = theta

    pl.semaphore_wait(barrier, len(peers))

    sends = []

    def send(src, dst, ss, rs, dev):
        cp = pltpu.make_async_remote_copy(src_ref=src, dst_ref=dst, send_sem=ss, recv_sem=rs, device_id=dev, device_id_type=MESH)
        cp.start()
        sends.append(cp)

    def arrived(dst, rs):
        pltpu.make_async_remote_copy(src_ref=dst, dst_ref=dst, send_sem=rs, recv_sem=rs, device_id=sib, device_id_type=MESH).wait_recv()

    own = thg.at[z, y, c]
    for k in Z_ORDER:
        send(own, own, gz_s.at[k], gz_r.at[k], at(zs[k], y, c))

    def to_y(k):
        part = thg.at[lax.rem(z + NZ - k, NZ), y, c]
        for j in (2, 1, 3):
            send(part, part, gy_s.at[j, k], gy_r.at[j, k], at(z, ys[j], c))

    to_y(0)
    for k in (2, 1, 3):
        send(thx.at[x], thx.at[x], tx_s.at[k], tx_r.at[k], (xs[k], dp))

    bins = bin_ref[...]
    off = jnp.zeros(bins.shape, F32)
    for b in range(bo_ref.shape[0]):
        off = jnp.where(bins == b, bo_ref[b], off)
    counts = cnt_ref[...]
    table = jnp.zeros(counts.shape, F32)
    for n in range(2, 8):
        table = jnp.where(counts == n, math.lgamma(n + 1.0), table)
    log_factorial = jnp.sum(table)
    cntf = counts.astype(F32)
    for i in range(n_rec // 128):
        rows = pl.ds(128 * i, 128)
        offb[rows, :] = jnp.broadcast_to(off[i : i + 1, :], (128, 128)).T
        cntb[rows, :] = jnp.broadcast_to(cntf[i : i + 1, :], (128, 128)).T

    def transpose_block(i):
        loads[i].wait()
        rect[:, :, :, pl.ds(i * blk, blk)] = rec[pl.ds(i * blk, blk), :].T.reshape(NZ, NY, 64, blk)

    for i, k in enumerate(Z_ARRIVE):
        arrived(thg.at[lax.rem(z + NZ - k, NZ), y, c], gz_r.at[k])
        to_y(k)
        transpose_block(i)
    send(thg.at[:, y, c], thg.at[:, y, c], gc_s.at[0], gc_r.at[0], sib)
    transpose_block(7)

    offs = offs_ref[...].astype(F32)
    upper = (lax.broadcasted_iota(jnp.int32, (128, 128), 0) <= lax.broadcasted_iota(jnp.int32, (128, 128), 1)).astype(F32).astype(BF16)
    within = jnp.dot(offs.astype(BF16), upper, preferred_element_type=F32)
    slots = jnp.concatenate([slot_ref[pl.ds(x * 4 + q, 1), :] for q in range(4)], axis=1).astype(F32)
    before = jnp.zeros((1, 1), F32)
    for i in range(offs.shape[0]):
        upto = within[i : i + 1, :] + before
        start = upto - offs[i : i + 1, :]
        upto_b = jnp.broadcast_to(upto, (128, 128)).T
        start_b = jnp.broadcast_to(start, (128, 128)).T
        for q in range(4):
            lanes = slice(128 * q, 128 * q + 128)
            hit = (slots[:, lanes] >= start_b) & (slots[:, lanes] < upto_b)
            sel[128 * i : 128 * i + 128, lanes] = jnp.where(hit, 1.0, 0.0).astype(BF16)
        before = before + within[i : i + 1, 127:128]

    for j in (1, 3, 2):
        yy = lax.rem(y + NY - j, NY)
        for k in range(NZ):
            arrived(thg.at[lax.rem(z + NZ - k, NZ), yy, c], gy_r.at[j, k])
        send(thg.at[:, yy, c], thg.at[:, yy, c], gc_s.at[j], gc_r.at[j], sib)
    for j in (0, 1, 3, 2):
        yy = lax.rem(y + NY - j, NY)
        arrived(thg.at[:, yy, 1 - c], gc_r.at[j])

    ll_own[...] = jnp.full(ll_own.shape, -log_factorial / 8.0, F32)

    @pl.loop(0, n_rec // 512)
    def _(i):
        rows = pl.ds(pl.multiple_of(i * 512, 512), 512)
        prod = jnp.dot(rec[rows, :], thg[...].reshape(n_feat, n_part), preferred_element_type=F32)
        o, t = offb[rows, :], cntb[rows, :]
        for q in range(n_part // 128):
            lanes = slice(128 * q, 128 * q + 128)
            lin = prod[:, lanes] * scale_in + o
            inten = jnp.exp(lin)
            ll_own[:, lanes] += jnp.sum((t * lin - inten).reshape(64, 8, 128), axis=0)
            res[rows, lanes] = (t - inten).astype(BF16)

    send(ll_own, ll_c, lc_s, lc_r, sib)

    def after_c(s):
        j = Y_STEPS[s]
        arrived(rcv_c.at[s], c_r.at[s])
        total = scf[s, :, c] + rcv_c[s].astype(F32)
        if j == 0:
            return total
        snd_y[s] = total.astype(BF16)
        send(snd_y.at[s], rcv_y.at[s], y_s.at[s], y_r.at[s], at(z, ys[j], c))

    for s, j in enumerate(Y_STEPS):
        part = jnp.dot(rect[:, ys[j]].reshape(512, n_rec), res[...], preferred_element_type=F32)
        scf[s] = part.reshape(NZ, 2, 32, n_part)
        snd_c[s] = scf[s, :, 1 - c].astype(BF16)
        send(snd_c.at[s], rcv_c.at[s], c_s.at[s], c_r.at[s], sib)
        if s == 0:
            arrived(ll_c, lc_r)
            ll_y[y] = ll_own[...] + ll_c[...]
            for k in (2, 1, 3):
                send(ll_y.at[y], ll_y.at[y], ly_s.at[k], ly_r.at[k], at(z, ys[k], c))
        else:
            after_c(s - 1)
    for k in (1, 3, 2):
        arrived(ll_y.at[lax.rem(y + NY - k, NY)], ly_r.at[k])
    ll_z[z] = (ll_y[0] + ll_y[1]) + (ll_y[2] + ll_y[3])
    for k in Z_ORDER:
        send(ll_z.at[z], ll_z.at[z], lz_s.at[k], lz_r.at[k], at(zs[k], y, c))
    total = after_c(3)
    for s in range(3):
        arrived(rcv_y.at[s], y_r.at[s])
        total = total + rcv_y[s].astype(F32)
    scf[0, :, 0] = total
    snd_z[...] = total.astype(BF16)
    for k in Z_ORDER:
        send(snd_z.at[zs[k]], rcv_z.at[k], z_s.at[k], z_r.at[k], at(zs[k], y, c))

    for k in (1, 3, 2):
        arrived(thx.at[lax.rem(x + NX - k, NX)], tx_r.at[k])
    everyone = jnp.concatenate([thx[q] for q in range(NX)], axis=1)
    hi = everyone.astype(BF16)
    rest = everyone - hi.astype(F32)
    mid = rest.astype(BF16)
    lo = (rest - mid.astype(F32)).astype(BF16)
    taken = jnp.dot(jnp.concatenate([hi, mid, lo], axis=0), sel[...], preferred_element_type=F32)
    taken = taken[0:32] + taken[32:64] + taken[64:96]
    step = step_ref[0]
    root = jnp.sqrt(jnp.full((1, 1), step, F32))
    base[...] = (1.0 - 0.5 * step) * taken + root * nz_ref[...]

    for k in Z_ARRIVE:
        arrived(ll_z.at[lax.rem(z + NZ - k, NZ)], lz_r.at[k])
    ll_x[x] = ((ll_z[0] + ll_z[1]) + (ll_z[2] + ll_z[3])) + ((ll_z[4] + ll_z[5]) + (ll_z[6] + ll_z[7]))
    for k in (2, 1, 3):
        send(ll_x.at[x], ll_x.at[x], lx_s.at[k], lx_r.at[k], (xs[k], dp))

    score = scf[0, z, 0]
    for k in Z_ARRIVE:
        arrived(rcv_z.at[k], z_r.at[k])
        score = score + rcv_z[k].astype(F32)
    scx[x] = score.astype(BF16)
    for k in (2, 1, 3):
        send(scx.at[x], scx.at[x], x_s.at[k], x_r.at[k], (xs[k], dp))

    for k in (1, 3, 2):
        arrived(ll_x.at[lax.rem(x + NX - k, NX)], lx_r.at[k])
    loglik = jnp.concatenate([jnp.sum(ll_x[q], axis=0, keepdims=True) for q in range(NX)], axis=0)
    log_weight = tstep_ref[0] * temper_scale * loglik
    peak = jnp.max(log_weight, axis=(0, 1), keepdims=True)
    shifted = jnp.exp(log_weight - peak)
    weight_sum = jnp.sum(shifted, axis=(0, 1), keepdims=True)
    weight_square = jnp.sum(shifted * shifted, axis=(0, 1), keepdims=True)
    le_ref[...] = peak + jnp.log(weight_sum) - math.log(NX * n_part)
    ess_ref[...] = weight_sum * weight_sum / (weight_square * (NX * n_part))

    for k in (1, 3, 2):
        arrived(scx.at[lax.rem(x + NX - k, NX)], x_r.at[k])
    scores = jnp.concatenate([scx[q] for q in range(NX)], axis=1)
    taken = jnp.dot(scores, sel[...], preferred_element_type=F32)
    out_ref[...] = base[...] + (0.5 * step * tlev_ref[0] * (temper_scale * scale_in)) * taken

    for cp in sends:
        cp.wait_send()


def on_device(records, counts_obs, exposure_bin, bin_offset, theta, noise, offspring, slot_order, temper_step, temper_level, step_size):
    n_rec, n_feat = records.shape
    n_part, cols = theta.shape
    vmem, smem = pl.BlockSpec(memory_space=pltpu.VMEM), pl.BlockSpec(memory_space=pltpu.SMEM)
    dma = pltpu.SemaphoreType.DMA
    blocks = (NZ, cols, n_part)
    scratch = [
        pltpu.VMEM((n_rec, n_feat), BF16),
        pltpu.VMEM((NZ, NY, 64, n_rec), BF16),
        pltpu.VMEM((NZ, NY, 2, cols, n_part), BF16),
        pltpu.VMEM((n_rec, n_part), BF16),
        pltpu.VMEM((n_rec, 128), F32),
        pltpu.VMEM((n_rec, 128), F32),
        pltpu.VMEM((NX * n_part, n_part), BF16),
        pltpu.VMEM((NX, cols, n_part), F32),
        pltpu.VMEM((cols, n_part), F32),
        pltpu.VMEM((4, NZ, 2, cols, n_part), F32),
        pltpu.VMEM((4,) + blocks, BF16),
        pltpu.VMEM((4,) + blocks, BF16),
        pltpu.VMEM((3,) + blocks, BF16),
        pltpu.VMEM((3,) + blocks, BF16),
        pltpu.VMEM(blocks, BF16),
        pltpu.VMEM(blocks, BF16),
        pltpu.VMEM((NX, cols, n_part), BF16),
        pltpu.VMEM((8, n_part), F32),
        pltpu.VMEM((8, n_part), F32),
        pltpu.VMEM((NY, 8, n_part), F32),
        pltpu.VMEM((NZ, 8, n_part), F32),
        pltpu.VMEM((NX, 8, n_part), F32),
        dma((8,)),
        dma((NZ,)), dma((NZ,)),
        dma((NY, NZ)), dma((NY, NZ)),
        dma((NY,)), dma((NY,)),
        dma((NX,)), dma((NX,)),
        dma((4,)), dma((4,)),
        dma((4,)), dma((4,)),
        dma((NZ,)), dma((NZ,)),
        dma((NX,)), dma((NX,)),
        dma, dma,
        dma((NY,)), dma((NY,)),
        dma((NZ,)), dma((NZ,)),
        dma((NX,)), dma((NX,)),
    ]
    moved, le, ess = pl.pallas_call(
        kernel,
        out_shape=(
            jax.ShapeDtypeStruct((cols, n_part), F32),
            jax.ShapeDtypeStruct((1, 1), F32),
            jax.ShapeDtypeStruct((1, 1), F32),
        ),
        in_specs=[pl.BlockSpec(memory_space=pl.ANY), vmem, vmem, smem, vmem, vmem, vmem, vmem, smem, smem, smem],
        out_specs=(vmem, vmem, vmem),
        scratch_shapes=scratch,
        compiler_params=pltpu.CompilerParams(collective_id=0, has_side_effects=True, vmem_limit_bytes=56 << 20),
        cost_estimate=pl.CostEstimate(flops=4 * n_rec * n_feat * n_part, bytes_accessed=2 * n_rec * n_feat, transcendentals=n_rec * n_part),
    )(
        records, counts_obs.reshape(-1, 128), exposure_bin.reshape(-1, 128), bin_offset, theta.T, noise.T,
        offspring.reshape(-1, 128), slot_order.reshape(-1, 128),
        temper_step.reshape(1), temper_level.reshape(1), step_size.reshape(1),
    )
    return moved.T, le[0, 0], ess[0, 0]


def solution(mesh):
    in_specs = (P("dp", None), P("dp"), P("dp"), P(), P("dom", "dp"), P("dom", "dp"), P(), P(), P(), P(), P())
    out_specs = (P("dom", "dp"), P(), P())
    return jax.shard_map(on_device, mesh=mesh, in_specs=in_specs, out_specs=out_specs, check_vma=False)
```

time: 309 us -> 75.7 us (0.24)
  blocking collectives: 171 us -> 0 us
  waiting for transfers between devices: 81.3 us -> 0 us
  Pallas kernels: 0 us -> 67.1 us
  between operations: 21.7 us -> 6.01 us
  matrix products: 15.3 us -> 0 us
  local copies, waits for them, and re-layouts: 10.5 us -> 1.47 us
  other arithmetic: 8.22 us -> 0 us
    psum x2 -> x0, blocking collectives: 135 us -> none  [the longest x1 124 us: on_device(): loglik = lax.psum(local_loglik, 'dp')]
    all_gather x1 -> x0, waiting for transfers between devices: 81.3 us -> none  [on_device(): gathered = lax.all_gather(theta_low, 'dp', axis=1, tiled=True)]
    pallas_call x0 -> x1, Pallas kernels: none -> 67.1 us  [on_device(): pl.pallas_call(kernel, out_shape=(jax.ShapeDtypeStruct((cols, n_part), F3...]
    all_gather x2 -> x0, blocking collectives: 26.7 us -> none  [the longest x1 15.5 us: on_device(): lax.all_gather(theta, 'dom', axis=0, tiled=True)]
    dot_general x2 -> x0, matrix products: 15.3 us -> none  [the longest x1 8.2 us: on_device(): lax.dot_general(records, gathered, (((1,), (1,)), ((), ())), preferred_el...]
    pmax x1 -> x0, blocking collectives: 8.96 us -> none  [on_device(): peak_value = lax.pmax(jnp.max(log_weight), 'dom')]
    unnamed x14 -> x1, local copies, waits for them, and re-layouts: 7.14 us -> 1.47 us
    reduce_sum x4 -> x0, other arithmetic: 3.39 us -> none  [the longest x1 1.26 us: on_device(): jnp.sum(shifted * shifted)]
  transfers between devices with their start and end apart: 2 -> 0, of which waited for: 1 -> 0; matrix products, arithmetic and copies ran while one was open for 3% -> 0% of each run, Pallas kernels for 0% -> 0%
where the time goes in v1:
time: 75.7 us; the launch traced here: 74.6 us
  Pallas kernels  67.1 us (89%)
  between operations  6.01 us (8%)
  local copies, waits for them, and re-layouts  1.47 us (2%)
    pallas_call x1, Pallas kernels, on_device(): pl.pallas_call(kernel, out_shape=(jax.ShapeDtypeStruct((cols, n_part), F3...  67.1 us

profile of v1, /device:TPU:2, one launch (start us, length us, event | category | flops | bytes accessed | tf_op | source)
XLA Modules:
  0.0 74.6 jit_solution(10097527628185135564)
XLA Ops:
  2.6 67.1 %shard_map.130 = (f32[32,512]{1,0:T(8,128)}, f32[1,1]{1,0:T(1,128)}, f32[1,1]{1,0:T(1,128)}) custom-call(bf16[2048,2048]{1,0:T(8,128)(2,1)} %rec_hbm.1, s32[16,128]{1,0:T(8,128)} %bitcast.18, s32[16,128]{1,0:T(8,128)} %bitcast.19, f32[64]{0:T(128)} %bo_ref.1, f32[32,512]{1,0:T(8,128)} %bitcast.16, f32[32,512]{1,0:T(8,128)} %bitcast.17, s32[16,128]{1,0:T(8,128)} %bitcast.20, ...), custom_call_target="tpu_custom_call" | custom-call | flops 8589934592 | bytes 8388608 | tf_op jit(solution)/shard_map/pallas_call | solution.py:277
  69.7 1.5 %copy.20 = f32[512,32]{0,1:T(8,128)} copy(f32[512,32]{0,1:T(8,128)} %bitcast.15) | data formatting | bytes 131072

commit v2 on v1

v2 whole, which is shorter than its diff:
```python
import math

import jax
import jax.numpy as jnp
from jax import lax
from jax.experimental import pallas as pl
from jax.experimental.pallas import tpu as pltpu
from jax.sharding import PartitionSpec as P

F32, BF16 = jnp.float32, jnp.bfloat16
MESH = pl.DeviceIdType.MESH
NZ, NY, NX, NH = 8, 4, 4, 2
NEAR = (1, 7)
FAR = (2, 6, 3, 5, 4)
SCORE_STEPS = ((4, 3), (5, 2), (6, 1), (7, 0))


def kernel(
    rec_hbm, cnt_hbm, bin_hbm, bo_hbm, th_hbm, nz_hbm, offs_hbm, slot_hbm, tstep_hbm, tlev_hbm, step_hbm,
    out_ref, le_ref, ess_ref,
    rec, rect, thg, res, offb, cntb, sel, thx, acc, scf, snd_c, rcv_c, snd_n, rcv_n, snd_y, rcv_y, snd_z, rcv_z, scx,
    ll_own, ll_c, ll_y, ll_z, ll_x, cnt_v, bin_v, th_v, nz_v, offs_v, slot_v, bo_s, tstep_s, tlev_s, step_s,
    rec_sem, in_sem, sent, gz_r, gy_r, gc_r, tx_r, c_r, n_r, y_r, z_r, x_r, lc_r, ly_r, lz_r, lx_r,
):
    x = lax.axis_index("dom")
    dp = lax.axis_index("dp")
    z, y, c = dp // 8, (dp // 2) % 4, dp % 2
    n_rec, n_feat = rec.shape
    n_part = th_v.shape[1]
    half = n_part // NH
    scale_in = 1.0 / math.sqrt(n_feat)
    temper_scale = math.sqrt(n_feat / (n_rec * NZ * NY * 2))

    def at(zz, yy, cc):
        return (x, zz * 8 + yy * 2 + cc)

    sib = at(z, y, 1 - c)
    zs = [lax.rem(z + k, NZ) for k in range(NZ)]
    ys = [lax.rem(y + k, NY) for k in range(NY)]
    xs = [lax.rem(x + k, NX) for k in range(NX)]
    z_from = [lax.rem(z + NZ - k, NZ) for k in range(NZ)]
    y_from = [lax.rem(y + NY - k, NY) for k in range(NY)]
    x_from = [lax.rem(x + NX - k, NX) for k in range(NX)]

    barrier = pltpu.get_barrier_semaphore()
    peers = [at(zs[k], y, c) for k in FAR[::-1] + NEAR] + [at(z, ys[k], c) for k in (2, 1, 3)] + [(xs[k], dp) for k in (2, 1, 3)] + [sib]
    for peer in peers:
        pl.semaphore_signal(barrier, inc=1, device_id=peer, device_id_type=MESH)

    def load(src, dst, sem):
        cp = pltpu.make_async_copy(src, dst, sem)
        cp.start()
        return cp

    th_in = load(th_hbm, th_v, in_sem.at[0])
    small = [
        load(s, d, in_sem.at[1 + i])
        for i, (s, d) in enumerate(
            ((bo_hbm, bo_s), (bin_hbm, bin_v), (cnt_hbm, cnt_v), (nz_hbm, nz_v), (offs_hbm, offs_v), (slot_hbm, slot_v),
             (tstep_hbm, tstep_s), (tlev_hbm, tlev_s), (step_hbm, step_s))
        )
    ]
    blk = n_rec // 4
    loads = [load(rec_hbm.at[pl.ds(i * blk, blk)], rec.at[pl.ds(i * blk, blk)], rec_sem.at[i]) for i in range(4)]

    th_in.wait()
    theta = th_v[...]
    for h in range(NH):
        thg[h, z, y, c] = theta[:, h * half : (h + 1) * half].astype(BF16)
    thx[x] = theta
    for cp in small:
        cp.wait()

    pl.semaphore_wait(barrier, len(peers))

    sends = []

    def send(src, dst, rs, dev):
        cp = pltpu.make_async_remote_copy(src_ref=src, dst_ref=dst, send_sem=sent, recv_sem=rs, device_id=dev, device_id_type=MESH)
        cp.start()
        sends.append(math.prod(src.shape) * src.dtype.itemsize)

    def arrived(dst, rs):
        pltpu.make_async_remote_copy(src_ref=dst, dst_ref=dst, send_sem=rs, recv_sem=rs, device_id=sib, device_id_type=MESH).wait_recv()

    def to_y(h, k):
        part = thg.at[h, z_from[k], y, c]
        for j in (2, 1, 3):
            send(part, part, gy_r.at[h, k], at(z, ys[j], c))

    def to_near(h):
        arrived(thg.at[h, z, pl.ds(0, 3), c], gy_r.at[h, 0])
        for j in (1, 3, 2):
            part = thg.at[h, z, y_from[j], c]
            for k in NEAR:
                send(part, part, gz_r.at[h, k], at(zs[k], y, c))

    def to_sib(h, k):
        if k in NEAR:
            arrived(thg.at[h, z_from[k], :, c], gz_r.at[h, k])
        elif k in FAR:
            arrived(thg.at[h, z_from[k], pl.ds(0, 3), c], gy_r.at[h, k])
        part = thg.at[h, z_from[k], :, c]
        send(part, part, gc_r.at[h], sib)

    def gathered(h):
        arrived(thg.at[h, :, :, c], gc_r.at[h])

    for h in range(NH):
        part = thg.at[h, z, y, c]
        for k in FAR + NEAR:
            send(part, part, gz_r.at[h, k], at(zs[k], y, c))
        to_y(h, 0)
    for k in (2, 1, 3):
        send(thx.at[x], thx.at[x], tx_r, (xs[k], dp))

    bins = bin_v[...]
    off = jnp.zeros(bins.shape, F32)
    for b in range(bo_s.shape[0]):
        off = jnp.where(bins == b, bo_s[b], off)
    counts = cnt_v[...]
    table = jnp.zeros(counts.shape, F32)
    for n in range(2, 8):
        table = jnp.where(counts == n, math.lgamma(n + 1.0), table)
    log_factorial = jnp.sum(table)
    cntf = counts.astype(F32)
    for i in range(n_rec // 128):
        rows = pl.ds(128 * i, 128)
        offb[rows, :] = jnp.broadcast_to(off[i : i + 1, :], (128, 128)).T
        cntb[rows, :] = jnp.broadcast_to(cntf[i : i + 1, :], (128, 128)).T

    def transpose_block(i):
        loads[i].wait()
        rect[:, :, :, pl.ds(i * blk, blk)] = rec[pl.ds(i * blk, blk), :].T.reshape(NZ, NY, 64, blk)

    for i in range(2):
        transpose_block(i)
    to_near(0)
    to_near(1)
    for h in range(NH):
        for k in FAR:
            arrived(thg.at[h, z_from[k], y, c], gz_r.at[h, k])
            to_y(h, k)
        to_sib(h, 0)
    for i in range(2, 4):
        transpose_block(i)

    ll_own[...] = jnp.full(ll_own.shape, -log_factorial / 8.0, F32)

    def matmul1(h, i):
        rows = pl.ds(i * 512, 512)
        prod = jnp.dot(rec[rows, :], thg[h].reshape(n_feat, half), preferred_element_type=F32)
        o, t = offb[rows, :], cntb[rows, :]
        for q in range(half // 128):
            lanes = slice(128 * q, 128 * q + 128)
            out_lanes = slice(h * half + 128 * q, h * half + 128 * q + 128)
            lin = prod[:, lanes] * scale_in + o
            inten = jnp.exp(lin)
            ll_own[:, out_lanes] += jnp.sum((t * lin - inten).reshape(64, 8, 128), axis=0)
            res[h, rows, lanes] = (t - inten).astype(BF16)

    def matmul2(h, s):
        for i, k in enumerate(SCORE_STEPS[s]):
            part = jnp.dot(rect[zs[k]].reshape(256, n_rec), res[h], preferred_element_type=F32)
            scf[h, k] = part.reshape(NY, 2, 32, half)
            snd_c[h, s, i] = scf[h, k, :, 1 - c].astype(BF16)
        send(snd_c.at[h, s], rcv_c.at[h, s], c_r.at[h, s], sib)

    def y_send(h, k):
        for j in (2, 1, 3):
            send(snd_y.at[h, k, ys[j]], rcv_y.at[h, k, j], y_r.at[h, k], at(z, ys[j], c))

    def chip_sum(h, s):
        arrived(rcv_c.at[h, s], c_r.at[h, s])
        for i, k in enumerate(SCORE_STEPS[s]):
            total = scf[h, k, :, c] + rcv_c[h, s, i].astype(F32)
            if k in NEAR:
                snd_n[h, k // 7] = total.astype(BF16)
                send(snd_n.at[h, k // 7], rcv_n.at[h, k // 7], n_r.at[h], at(zs[k], y, c))
            else:
                scf[h, k, :, 0] = total
                if k:
                    snd_y[h, k] = total.astype(BF16)
                    y_send(h, k)

    def near_sum(h):
        total = scf[h, 0, :, 0]
        arrived(rcv_n.at[h], n_r.at[h])
        for i in range(2):
            total = total + rcv_n[h, i].astype(F32)
        scf[h, 0, :, 0] = total
        snd_y[h, 0] = total.astype(BF16)
        y_send(h, 0)

    def y_sum(h, k):
        total = scf[h, k, y, 0]
        arrived(rcv_y.at[h, k, pl.ds(0, 3)], y_r.at[h, k])
        for j in (1, 3, 2):
            total = total + rcv_y[h, k, j].astype(F32)
        return total

    def far_send(h, k):
        snd_z[h, k] = y_sum(h, k).astype(BF16)
        send(snd_z.at[h, k], rcv_z.at[h, k], z_r.at[h], at(zs[k], y, c))

    def z_sum(h):
        score = y_sum(h, 0)
        arrived(rcv_z.at[h, pl.ds(0, 5)], z_r.at[h])
        for k in FAR:
            score = score + rcv_z[h, k].astype(F32)
        scx[h, x] = score.astype(BF16)
        for k in (2, 1, 3):
            send(scx.at[h, x], scx.at[h, x], x_r.at[h], (xs[k], dp))

    def resampled_score(h):
        arrived(scx.at[h, pl.ds(0, 3)], x_r.at[h])
        scores = jnp.concatenate([scx[h, q] for q in range(NX)], axis=1)
        return jnp.dot(scores, sel[:, h].reshape(NX * half, n_part), preferred_element_type=F32)

    for k in FAR + NEAR:
        to_sib(0, k)
    gathered(0)
    for i in range(4):
        matmul1(0, i)
    for k in (2, 6):
        to_sib(1, k)
    for i in range(4):
        matmul2(0, i)
        if i:
            chip_sum(0, i - 1)
    chip_sum(0, 3)
    for k in (3, 5, 4) + NEAR:
        to_sib(1, k)
    gathered(1)
    for i in range(4):
        matmul1(1, i)
    send(ll_own, ll_c, lc_r, sib)
    for i in range(4):
        matmul2(1, i)
        if i:
            chip_sum(1, i - 1)
        else:
            arrived(ll_c, lc_r)
            ll_y[y] = ll_own[...] + ll_c[...]
            for k in (2, 1, 3):
                send(ll_y.at[y], ll_y.at[y], ly_r, at(z, ys[k], c))
        if i == 2:
            near_sum(0)
    chip_sum(1, 3)
    for k in (4, 3, 5, 2, 6):
        far_send(0, k)
    near_sum(1)
    arrived(ll_y.at[pl.ds(0, 3)], ly_r)
    ll_z[z] = (ll_y[0] + ll_y[1]) + (ll_y[2] + ll_y[3])
    for k in FAR + NEAR:
        send(ll_z.at[z], ll_z.at[z], lz_r, at(zs[k], y, c))

    offs = offs_v[...].astype(F32)
    upper = (lax.broadcasted_iota(jnp.int32, (128, 128), 0) <= lax.broadcasted_iota(jnp.int32, (128, 128), 1)).astype(F32).astype(BF16)
    within = jnp.dot(offs.astype(BF16), upper, preferred_element_type=F32)
    slots = jnp.concatenate([slot_v[pl.ds(x * 4 + q, 1), :] for q in range(4)], axis=1).astype(F32)
    before = jnp.zeros((1, 1), F32)
    for i in range(offs.shape[0]):
        upto = within[i : i + 1, :] + before
        start = upto - offs[i : i + 1, :]
        upto_b = jnp.broadcast_to(upto, (128, 128)).T
        start_b = jnp.broadcast_to(start, (128, 128)).T
        for q in range(4):
            lanes = slice(128 * q, 128 * q + 128)
            hit = (slots[:, lanes] >= start_b) & (slots[:, lanes] < upto_b)
            sel[i // 4, (i % 4) // 2, 128 * (i % 2) : 128 * (i % 2) + 128, lanes] = jnp.where(hit, 1.0, 0.0).astype(BF16)
        before = before + within[i : i + 1, 127:128]

    arrived(thx.at[pl.ds(0, 3)], tx_r)
    everyone = jnp.concatenate([thx[q] for q in range(NX)], axis=1)
    hi = everyone.astype(BF16)
    rest = everyone - hi.astype(F32)
    mid = rest.astype(BF16)
    lo = (rest - mid.astype(F32)).astype(BF16)
    taken = jnp.dot(jnp.concatenate([hi, mid, lo], axis=0), sel[...].reshape(NX * n_part, n_part), preferred_element_type=F32)
    taken = taken[0:32] + taken[32:64] + taken[64:96]
    step = step_s[0]
    root = jnp.sqrt(jnp.full((1, 1), step, F32))
    acc[...] = (1.0 - 0.5 * step) * taken + root * nz_v[...]
    gain = 0.5 * step * tlev_s[0] * (temper_scale * scale_in)

    for k in (4, 3, 5, 2, 6):
        far_send(1, k)
    z_sum(0)
    arrived(ll_z.at[pl.ds(0, 7)], lz_r)
    ll_x[x] = ((ll_z[0] + ll_z[1]) + (ll_z[2] + ll_z[3])) + ((ll_z[4] + ll_z[5]) + (ll_z[6] + ll_z[7]))
    for k in (2, 1, 3):
        send(ll_x.at[x], ll_x.at[x], lx_r, (xs[k], dp))
    acc[...] += gain * resampled_score(0)
    z_sum(1)

    arrived(ll_x.at[pl.ds(0, 3)], lx_r)
    loglik = jnp.concatenate([jnp.sum(ll_x[q], axis=0, keepdims=True) for q in range(NX)], axis=0)
    log_weight = tstep_s[0] * temper_scale * loglik
    peak = jnp.max(log_weight, axis=(0, 1), keepdims=True)
    shifted = jnp.exp(log_weight - peak)
    weight_sum = jnp.sum(shifted, axis=(0, 1), keepdims=True)
    weight_square = jnp.sum(shifted * shifted, axis=(0, 1), keepdims=True)
    le_ref[...] = peak + jnp.log(weight_sum) - math.log(NX * n_part)
    ess_ref[...] = weight_sum * weight_sum / (weight_square * (NX * n_part))

    out_ref[...] = acc[...] + gain * resampled_score(1)

    everything = rec.at[pl.ds(0, sum(sends) // (2 * n_feat))]
    pltpu.make_async_remote_copy(src_ref=everything, dst_ref=everything, send_sem=sent, recv_sem=sent, device_id=sib, device_id_type=MESH).wait_send()


def hand_over(*refs):
    for i in range(3):
        refs[3 + i][...] = refs[i][...]


def on_device(records, counts_obs, exposure_bin, bin_offset, theta, noise, offspring, slot_order, temper_step, temper_level, step_size):
    n_rec, n_feat = records.shape
    n_part, cols = theta.shape
    half = n_part // NH
    vmem, anywhere = pl.BlockSpec(memory_space=pltpu.VMEM), pl.BlockSpec(memory_space=pl.ANY)
    dma = pltpu.SemaphoreType.DMA
    counts_obs, exposure_bin, offspring, slot_order = (a.reshape(-1, 128) for a in (counts_obs, exposure_bin, offspring, slot_order))
    scratch = [
        pltpu.VMEM((n_rec, n_feat), BF16),
        pltpu.VMEM((NZ, NY, 64, n_rec), BF16),
        pltpu.VMEM((NH, NZ, NY, 2, cols, half), BF16),
        pltpu.VMEM((NH, n_rec, half), BF16),
        pltpu.VMEM((n_rec, 128), F32),
        pltpu.VMEM((n_rec, 128), F32),
        pltpu.VMEM((NX, NH, half, n_part), BF16),
        pltpu.VMEM((NX, cols, n_part), F32),
        pltpu.VMEM((cols, n_part), F32),
        pltpu.VMEM((NH, NZ, NY, 2, cols, half), F32),
        pltpu.VMEM((NH, 4, 2, NY, cols, half), BF16),
        pltpu.VMEM((NH, 4, 2, NY, cols, half), BF16),
        pltpu.VMEM((NH, 2, NY, cols, half), BF16),
        pltpu.VMEM((NH, 2, NY, cols, half), BF16),
        pltpu.VMEM((NH, NZ, NY, cols, half), BF16),
        pltpu.VMEM((NH, NZ, NY, cols, half), BF16),
        pltpu.VMEM((NH, NZ, cols, half), BF16),
        pltpu.VMEM((NH, NZ, cols, half), BF16),
        pltpu.VMEM((NH, NX, cols, half), BF16),
        pltpu.VMEM((8, n_part), F32),
        pltpu.VMEM((8, n_part), F32),
        pltpu.VMEM((NY, 8, n_part), F32),
        pltpu.VMEM((NZ, 8, n_part), F32),
        pltpu.VMEM((NX, 8, n_part), F32),
        pltpu.VMEM(counts_obs.shape, jnp.int32),
        pltpu.VMEM(exposure_bin.shape, jnp.int32),
        pltpu.VMEM((cols, n_part), F32),
        pltpu.VMEM((cols, n_part), F32),
        pltpu.VMEM(offspring.shape, jnp.int32),
        pltpu.VMEM(slot_order.shape, jnp.int32),
        pltpu.SMEM(bin_offset.shape, F32),
        pltpu.SMEM((1,), F32), pltpu.SMEM((1,), F32), pltpu.SMEM((1,), F32),
        dma((4,)), dma((10,)), dma,
        dma((NH, NZ)), dma((NH, NZ)), dma((NH,)), dma,
        dma((NH, 4)), dma((NH,)), dma((NH, NZ)), dma((NH,)), dma((NH,)),
        dma, dma, dma, dma,
    ]
    shapes = (
        jax.ShapeDtypeStruct((cols, n_part), F32),
        jax.ShapeDtypeStruct((1, 1), F32),
        jax.ShapeDtypeStruct((1, 1), F32),
    )
    results = pl.pallas_call(
        kernel,
        out_shape=shapes,
        in_specs=[anywhere] * 11,
        out_specs=(vmem, vmem, vmem),
        scratch_shapes=scratch,
        compiler_params=pltpu.CompilerParams(collective_id=0, has_side_effects=True, vmem_limit_bytes=60 << 20),
        cost_estimate=pl.CostEstimate(flops=4 * n_rec * n_feat * n_part, bytes_accessed=2 * n_rec * n_feat, transcendentals=n_rec * n_part),
    )(
        records, counts_obs, exposure_bin, bin_offset, theta.T, noise.T, offspring, slot_order,
        temper_step.reshape(1), temper_level.reshape(1), step_size.reshape(1),
    )
    moved, le, ess = pl.pallas_call(
        hand_over,
        out_shape=shapes,
        in_specs=[vmem] * 3,
        out_specs=(vmem,) * 3,
    )(*results)
    return moved.T, le[0, 0], ess[0, 0]


def solution(mesh):
    in_specs = (P("dp", None), P("dp"), P("dp"), P(), P("dom", "dp"), P("dom", "dp"), P(), P(), P(), P(), P())
    out_specs = (P("dom", "dp"), P(), P())
    return jax.shard_map(on_device, mesh=mesh, in_specs=in_specs, out_specs=out_specs, check_vma=False)
```

time: 75.7 us -> 60.3 us (0.80)
  Pallas kernels: 67.1 us -> 56.8 us
  between operations: 6.01 us -> 2.58 us
  local copies, waits for them, and re-layouts: 1.47 us -> 0 us
    pallas_call x1 -> x2, Pallas kernels: 67.1 us -> 56.8 us  [the longest x1 54.1 us: on_device(): pl.pallas_call(kernel, out_shape=shapes, in_specs=[anywhere] * 11, out_sp...]
    unnamed x1 -> x0, local copies, waits for them, and re-layouts: 1.47 us -> none
where the time goes in v2:
time: 60.3 us; the launch traced here: 59.4 us
  Pallas kernels  56.8 us (94%)
  between operations  2.58 us (4%)
    pallas_call x1, Pallas kernels, on_device(): pl.pallas_call(kernel, out_shape=shapes, in_specs=[anywhere] * 11, out_sp...  54.1 us
    pallas_call x1, Pallas kernels, on_device(): pl.pallas_call(hand_over, out_shape=shapes, in_specs=[vmem] * 3, out_spec...  2.72 us

profile of v2, /device:TPU:2, one launch (start us, length us, event | category | flops | bytes accessed | tf_op | source)
XLA Modules:
  0.0 59.4 jit_solution(13976879551512188648)
XLA Ops:
  2.6 54.1 %shard_map.130 = (f32[32,512]{1,0:T(8,128)}, f32[1,1]{1,0:T(1,128)}, f32[1,1]{1,0:T(1,128)}) custom-call(bf16[2048,2048]{1,0:T(8,128)(2,1)} %rec_hbm.1, s32[16,128]{1,0:T(8,128)} %bitcast.18, s32[16,128]{1,0:T(8,128)} %bitcast.19, f32[64]{0:T(128)} %bo_hbm.1, f32[32,512]{1,0:T(8,128)} %bitcast.15, f32[32,512]{1,0:T(8,128)} %bitcast.16, s32[16,128]{1,0:T(8,128)} %bitcast.20, ...), custom_call_target="tpu_custom_call" | custom-call | flops 8589934592 | bytes 8388608 | tf_op jit(solution)/shard_map/pallas_call | solution.py:368
  56.7 2.7 %shard_map.131 = (f32[32,512]{1,0:T(8,128)}, f32[1,1]{1,0:T(1,128)}, f32[1,1]{1,0:T(1,128)}) custom-call(f32[32,512]{1,0:T(8,128)} %get-tuple-element.9.refs_0_, f32[1,1]{1,0:T(1,128)} %get-tuple-element.10.refs_1_, f32[1,1]{1,0:T(1,128)} %get-tuple-element.11.refs_2_), custom_call_target="tpu_custom_call" | custom-call | tf_op jit(solution)/shard_map/pallas_call | solution.py:380

commit v3 on v2

--- a/solution.py
+++ b/solution.py
@@ -11,16 +11,16 @@
 MESH = pl.DeviceIdType.MESH
 NZ, NY, NX, NH = 8, 4, 4, 2
 NEAR = (1, 7)
-FAR = (2, 6, 3, 5, 4)
-SCORE_STEPS = ((4, 3), (5, 2), (6, 1), (7, 0))
+FAR = (2, 6, 4, 3, 5)
+SCORE_STEPS = ((4, 3), (1, 7), (5, 2), (6, 0))
 
 
 def kernel(
     rec_hbm, cnt_hbm, bin_hbm, bo_hbm, th_hbm, nz_hbm, offs_hbm, slot_hbm, tstep_hbm, tlev_hbm, step_hbm,
     out_ref, le_ref, ess_ref,
     rec, rect, thg, res, offb, cntb, sel, thx, acc, scf, snd_c, rcv_c, snd_n, rcv_n, snd_y, rcv_y, snd_z, rcv_z, scx,
-    ll_own, ll_c, ll_y, ll_z, ll_x, cnt_v, bin_v, th_v, nz_v, offs_v, slot_v, bo_s, tstep_s, tlev_s, step_s,
-    rec_sem, in_sem, sent, gz_r, gy_r, gc_r, tx_r, c_r, n_r, y_r, z_r, x_r, lc_r, ly_r, lz_r, lx_r,
+    ll_own, ll_rows, cnt_v, bin_v, th_v, nz_v, offs_v, slot_v, bo_s, tstep_s, tlev_s, step_s,
+    rec_sem, in_sem, sent, row_sent, x_sent, gz_r, gy_r, gc_r, tx_r, c_r, n_r, y_r, z_r, x_r, lc_r, ly_r, lz_r, lx_r,
 ):
     x = lax.axis_index("dom")
     dp = lax.axis_index("dp")
@@ -75,10 +75,14 @@
 
     sends = []
 
-    def send(src, dst, rs, dev):
-        cp = pltpu.make_async_remote_copy(src_ref=src, dst_ref=dst, send_sem=sent, recv_sem=rs, device_id=dev, device_id_type=MESH)
+    def send(src, dst, rs, dev, ss=None):
+        row = src.shape[-2] == 1
+        cp = pltpu.make_async_remote_copy(
+            src_ref=src, dst_ref=dst, send_sem=ss if ss is not None else row_sent if row else sent, recv_sem=rs, device_id=dev, device_id_type=MESH
+        )
         cp.start()
-        sends.append(math.prod(src.shape) * src.dtype.itemsize)
+        if not row and ss is None:
+            sends.append(math.prod(src.shape) * src.dtype.itemsize)
 
     def arrived(dst, rs):
         pltpu.make_async_remote_copy(src_ref=dst, dst_ref=dst, send_sem=rs, recv_sem=rs, device_id=sib, device_id_type=MESH).wait_recv()
@@ -138,12 +142,15 @@
     to_near(0)
     to_near(1)
     for h in range(NH):
-        for k in FAR:
+        for i, k in enumerate(FAR):
             arrived(thg.at[h, z_from[k], y, c], gz_r.at[h, k])
             to_y(h, k)
-        to_sib(h, 0)
-    for i in range(2, 4):
-        transpose_block(i)
+            if h == 0 and i in (1, 3):
+                transpose_block(2 + i // 2)
+            if h == 1:
+                to_sib(0, k)
+        if h == 0:
+            to_sib(0, 0)
 
     ll_own[...] = jnp.full(ll_own.shape, -log_factorial / 8.0, F32)
 
@@ -210,51 +217,48 @@
             score = score + rcv_z[h, k].astype(F32)
         scx[h, x] = score.astype(BF16)
         for k in (2, 1, 3):
-            send(scx.at[h, x], scx.at[h, x], x_r.at[h], (xs[k], dp))
+            send(scx.at[h, x], scx.at[h, x], x_r.at[h], (xs[k], dp), x_sent)
 
     def resampled_score(h):
         arrived(scx.at[h, pl.ds(0, 3)], x_r.at[h])
         scores = jnp.concatenate([scx[h, q] for q in range(NX)], axis=1)
         return jnp.dot(scores, sel[:, h].reshape(NX * half, n_part), preferred_element_type=F32)
 
-    for k in FAR + NEAR:
+    for k in NEAR:
         to_sib(0, k)
+    to_sib(1, 0)
     gathered(0)
     for i in range(4):
         matmul1(0, i)
-    for k in (2, 6):
+    for k in FAR + NEAR:
         to_sib(1, k)
     for i in range(4):
         matmul2(0, i)
         if i:
             chip_sum(0, i - 1)
     chip_sum(0, 3)
-    for k in (3, 5, 4) + NEAR:
-        to_sib(1, k)
     gathered(1)
     for i in range(4):
         matmul1(1, i)
-    send(ll_own, ll_c, lc_r, sib)
+    ll_rows[0] = jnp.sum(ll_own[...], axis=0, keepdims=True)
+    send(ll_rows.at[0], ll_rows.at[1], lc_r, sib)
     for i in range(4):
         matmul2(1, i)
         if i:
             chip_sum(1, i - 1)
         else:
-            arrived(ll_c, lc_r)
-            ll_y[y] = ll_own[...] + ll_c[...]
+            arrived(ll_rows.at[1], lc_r)
+            ll_rows[2 + y] = ll_rows[0] + ll_rows[1]
             for k in (2, 1, 3):
-                send(ll_y.at[y], ll_y.at[y], ly_r, at(z, ys[k], c))
-        if i == 2:
-            near_sum(0)
+                send(ll_rows.at[2 + y], ll_rows.at[2 + y], ly_r, at(z, ys[k], c))
     chip_sum(1, 3)
+    arrived(ll_rows.at[pl.ds(2, 3)], ly_r)
+    ll_rows[6 + z] = (ll_rows[2] + ll_rows[3]) + (ll_rows[4] + ll_rows[5])
+    for k in FAR + NEAR:
+        send(ll_rows.at[6 + z], ll_rows.at[6 + z], lz_r, at(zs[k], y, c))
+    near_sum(0)
     for k in (4, 3, 5, 2, 6):
         far_send(0, k)
-    near_sum(1)
-    arrived(ll_y.at[pl.ds(0, 3)], ly_r)
-    ll_z[z] = (ll_y[0] + ll_y[1]) + (ll_y[2] + ll_y[3])
-    for k in FAR + NEAR:
-        send(ll_z.at[z], ll_z.at[z], lz_r, at(zs[k], y, c))
-
     offs = offs_v[...].astype(F32)
     upper = (lax.broadcasted_iota(jnp.int32, (128, 128), 0) <= lax.broadcasted_iota(jnp.int32, (128, 128), 1)).astype(F32).astype(BF16)
     within = jnp.dot(offs.astype(BF16), upper, preferred_element_type=F32)
@@ -284,18 +288,20 @@
     acc[...] = (1.0 - 0.5 * step) * taken + root * nz_v[...]
     gain = 0.5 * step * tlev_s[0] * (temper_scale * scale_in)
 
+    near_sum(1)
     for k in (4, 3, 5, 2, 6):
         far_send(1, k)
+    arrived(ll_rows.at[pl.ds(6, 7)], lz_r)
+    rows = [ll_rows[6 + q] for q in range(NZ)]
+    ll_rows[14 + x] = ((rows[0] + rows[1]) + (rows[2] + rows[3])) + ((rows[4] + rows[5]) + (rows[6] + rows[7]))
+    for k in (2, 1, 3):
+        send(ll_rows.at[14 + x], ll_rows.at[14 + x], lx_r, (xs[k], dp))
     z_sum(0)
-    arrived(ll_z.at[pl.ds(0, 7)], lz_r)
-    ll_x[x] = ((ll_z[0] + ll_z[1]) + (ll_z[2] + ll_z[3])) + ((ll_z[4] + ll_z[5]) + (ll_z[6] + ll_z[7]))
-    for k in (2, 1, 3):
-        send(ll_x.at[x], ll_x.at[x], lx_r, (xs[k], dp))
     acc[...] += gain * resampled_score(0)
     z_sum(1)
 
-    arrived(ll_x.at[pl.ds(0, 3)], lx_r)
-    loglik = jnp.concatenate([jnp.sum(ll_x[q], axis=0, keepdims=True) for q in range(NX)], axis=0)
+    arrived(ll_rows.at[pl.ds(14, 3)], lx_r)
+    loglik = jnp.concatenate([ll_rows[14 + q] for q in range(NX)], axis=0)
     log_weight = tstep_s[0] * temper_scale * loglik
     peak = jnp.max(log_weight, axis=(0, 1), keepdims=True)
     shifted = jnp.exp(log_weight - peak)
@@ -306,6 +312,11 @@
 
     out_ref[...] = acc[...] + gain * resampled_score(1)
 
+    part = scx.at[:, pl.ds(0, 3)]
+    pltpu.make_async_remote_copy(src_ref=part, dst_ref=part, send_sem=x_sent, recv_sem=x_sent, device_id=sib, device_id_type=MESH).wait_send()
+    rows_sent = ll_rows.at[pl.ds(0, 14)]
+    pltpu.make_async_remote_copy(src_ref=rows_sent, dst_ref=rows_sent, send_sem=row_sent, recv_sem=row_sent, device_id=sib, device_id_type=MESH).wait_send()
+    assert sum(sends) % (32 * n_feat) == 0
     everything = rec.at[pl.ds(0, sum(sends) // (2 * n_feat))]
     pltpu.make_async_remote_copy(src_ref=everything, dst_ref=everything, send_sem=sent, recv_sem=sent, device_id=sib, device_id_type=MESH).wait_send()
 
@@ -343,10 +354,7 @@
         pltpu.VMEM((NH, NZ, cols, half), BF16),
         pltpu.VMEM((NH, NX, cols, half), BF16),
         pltpu.VMEM((8, n_part), F32),
-        pltpu.VMEM((8, n_part), F32),
-        pltpu.VMEM((NY, 8, n_part), F32),
-        pltpu.VMEM((NZ, 8, n_part), F32),
-        pltpu.VMEM((NX, 8, n_part), F32),
+        pltpu.VMEM((2 + NY + NZ + NX, 1, n_part), F32),
         pltpu.VMEM(counts_obs.shape, jnp.int32),
         pltpu.VMEM(exposure_bin.shape, jnp.int32),
         pltpu.VMEM((cols, n_part), F32),
@@ -355,7 +363,7 @@
         pltpu.VMEM(slot_order.shape, jnp.int32),
         pltpu.SMEM(bin_offset.shape, F32),
         pltpu.SMEM((1,), F32), pltpu.SMEM((1,), F32), pltpu.SMEM((1,), F32),
-        dma((4,)), dma((10,)), dma,
+        dma((4,)), dma((10,)), dma, dma, dma,
         dma((NH, NZ)), dma((NH, NZ)), dma((NH,)), dma,
         dma((NH, 4)), dma((NH,)), dma((NH, NZ)), dma((NH,)), dma((NH,)),
         dma, dma, dma, dma,

time: 60.3 us -> 57.7 us (0.957)
  the two profiles are of different devices: /device:TPU:2 before, /device:TPU:32 now
where the time goes in v3:
time: 57.7 us; the launch traced here: 57.5 us
  Pallas kernels  54.9 us (95%)
  between operations  2.58 us (4%)
    pallas_call x1, Pallas kernels, on_device(): pl.pallas_call(kernel, out_shape=shapes, in_specs=[anywhere] * 11, out_sp...  52.2 us
    pallas_call x1, Pallas kernels, on_device(): pl.pallas_call(hand_over, out_shape=shapes, in_specs=[vmem] * 3, out_spec...  2.72 us

profile of v3, /device:TPU:32, one launch (start us, length us, event | category | flops | bytes accessed | tf_op | source)
XLA Modules:
  0.0 57.5 jit_solution(5233742531219739210)
XLA Ops:
  2.6 52.2 %shard_map.130 = (f32[32,512]{1,0:T(8,128)}, f32[1,1]{1,0:T(1,128)}, f32[1,1]{1,0:T(1,128)}) custom-call(bf16[2048,2048]{1,0:T(8,128)(2,1)} %rec_hbm.1, s32[16,128]{1,0:T(8,128)} %bitcast.18, s32[16,128]{1,0:T(8,128)} %bitcast.19, f32[64]{0:T(128)} %bo_hbm.1, f32[32,512]{1,0:T(8,128)} %bitcast.15, f32[32,512]{1,0:T(8,128)} %bitcast.16, s32[16,128]{1,0:T(8,128)} %bitcast.20, ...), custom_call_target="tpu_custom_call" | custom-call | flops 8589934592 | bytes 8388608 | tf_op jit(solution)/shard_map/pallas_call | solution.py:376
  54.8 2.7 %shard_map.131 = (f32[32,512]{1,0:T(8,128)}, f32[1,1]{1,0:T(1,128)}, f32[1,1]{1,0:T(1,128)}) custom-call(f32[32,512]{1,0:T(8,128)} %get-tuple-element.9.refs_0_, f32[1,1]{1,0:T(1,128)} %get-tuple-element.10.refs_1_, f32[1,1]{1,0:T(1,128)} %get-tuple-element.11.refs_2_), custom_call_target="tpu_custom_call" | custom-call | tf_op jit(solution)/shard_map/pallas_call | solution.py:388

commit v4 on v3

--- a/solution.py
+++ b/solution.py
@@ -110,11 +110,13 @@
     def gathered(h):
         arrived(thg.at[h, :, :, c], gc_r.at[h])
 
-    for h in range(NH):
-        part = thg.at[h, z, y, c]
-        for k in FAR + NEAR:
-            send(part, part, gz_r.at[h, k], at(zs[k], y, c))
-        to_y(h, 0)
+    for ks in (FAR, NEAR):
+        for h in range(NH):
+            part = thg.at[h, z, y, c]
+            for k in ks:
+                send(part, part, gz_r.at[h, k], at(zs[k], y, c))
+            if ks == FAR:
+                to_y(h, 0)
     for k in (2, 1, 3):
         send(thx.at[x], thx.at[x], tx_r, (xs[k], dp))
 
@@ -227,38 +229,6 @@
     for k in NEAR:
         to_sib(0, k)
     to_sib(1, 0)
-    gathered(0)
-    for i in range(4):
-        matmul1(0, i)
-    for k in FAR + NEAR:
-        to_sib(1, k)
-    for i in range(4):
-        matmul2(0, i)
-        if i:
-            chip_sum(0, i - 1)
-    chip_sum(0, 3)
-    gathered(1)
-    for i in range(4):
-        matmul1(1, i)
-    ll_rows[0] = jnp.sum(ll_own[...], axis=0, keepdims=True)
-    send(ll_rows.at[0], ll_rows.at[1], lc_r, sib)
-    for i in range(4):
-        matmul2(1, i)
-        if i:
-            chip_sum(1, i - 1)
-        else:
-            arrived(ll_rows.at[1], lc_r)
-            ll_rows[2 + y] = ll_rows[0] + ll_rows[1]
-            for k in (2, 1, 3):
-                send(ll_rows.at[2 + y], ll_rows.at[2 + y], ly_r, at(z, ys[k], c))
-    chip_sum(1, 3)
-    arrived(ll_rows.at[pl.ds(2, 3)], ly_r)
-    ll_rows[6 + z] = (ll_rows[2] + ll_rows[3]) + (ll_rows[4] + ll_rows[5])
-    for k in FAR + NEAR:
-        send(ll_rows.at[6 + z], ll_rows.at[6 + z], lz_r, at(zs[k], y, c))
-    near_sum(0)
-    for k in (4, 3, 5, 2, 6):
-        far_send(0, k)
     offs = offs_v[...].astype(F32)
     upper = (lax.broadcasted_iota(jnp.int32, (128, 128), 0) <= lax.broadcasted_iota(jnp.int32, (128, 128), 1)).astype(F32).astype(BF16)
     within = jnp.dot(offs.astype(BF16), upper, preferred_element_type=F32)
@@ -288,6 +258,41 @@
     acc[...] = (1.0 - 0.5 * step) * taken + root * nz_v[...]
     gain = 0.5 * step * tlev_s[0] * (temper_scale * scale_in)
 
+    gathered(0)
+    for i in range(4):
+        matmul1(0, i)
+    for k in FAR + NEAR:
+        to_sib(1, k)
+    for i in range(4):
+        matmul2(0, i)
+        if i > 1:
+            chip_sum(0, i - 2)
+    gathered(1)
+    for i in range(4):
+        matmul1(1, i)
+        if i == 0:
+            chip_sum(0, 2)
+            chip_sum(0, 3)
+    ll_rows[0] = jnp.sum(ll_own[...], axis=0, keepdims=True)
+    send(ll_rows.at[0], ll_rows.at[1], lc_r, sib)
+    for i in range(4):
+        matmul2(1, i)
+        if i > 1:
+            chip_sum(1, i - 2)
+        if i == 1:
+            arrived(ll_rows.at[1], lc_r)
+            ll_rows[2 + y] = ll_rows[0] + ll_rows[1]
+            for k in (2, 1, 3):
+                send(ll_rows.at[2 + y], ll_rows.at[2 + y], ly_r, at(z, ys[k], c))
+    chip_sum(1, 2)
+    chip_sum(1, 3)
+    arrived(ll_rows.at[pl.ds(2, 3)], ly_r)
+    ll_rows[6 + z] = (ll_rows[2] + ll_rows[3]) + (ll_rows[4] + ll_rows[5])
+    for k in FAR + NEAR:
+        send(ll_rows.at[6 + z], ll_rows.at[6 + z], lz_r, at(zs[k], y, c))
+    near_sum(0)
+    for k in (4, 3, 5, 2, 6):
+        far_send(0, k)
     near_sum(1)
     for k in (4, 3, 5, 2, 6):
         far_send(1, k)

time: 57.7 us -> 56.8 us (0.984)
  the two profiles are of different devices: /device:TPU:32 before, /device:TPU:2 now
where the time goes in v4:
time: 56.8 us; the launch traced here: 56.6 us
  Pallas kernels  54.1 us (95%)
  between operations  2.58 us (5%)
    pallas_call x1, Pallas kernels, on_device(): pl.pallas_call(kernel, out_shape=shapes, in_specs=[anywhere] * 11, out_sp...  51.3 us
    pallas_call x1, Pallas kernels, on_device(): pl.pallas_call(hand_over, out_shape=shapes, in_specs=[vmem] * 3, out_spec...  2.72 us

profile of v4, /device:TPU:2, one launch (start us, length us, event | category | flops | bytes accessed | tf_op | source)
XLA Modules:
  0.0 56.6 jit_solution(13330093775031092465)
XLA Ops:
  2.6 51.3 %shard_map.130 = (f32[32,512]{1,0:T(8,128)}, f32[1,1]{1,0:T(1,128)}, f32[1,1]{1,0:T(1,128)}) custom-call(bf16[2048,2048]{1,0:T(8,128)(2,1)} %rec_hbm.1, s32[16,128]{1,0:T(8,128)} %bitcast.18, s32[16,128]{1,0:T(8,128)} %bitcast.19, f32[64]{0:T(128)} %bo_hbm.1, f32[32,512]{1,0:T(8,128)} %bitcast.15, f32[32,512]{1,0:T(8,128)} %bitcast.16, s32[16,128]{1,0:T(8,128)} %bitcast.20, ...), custom_call_target="tpu_custom_call" | custom-call | flops 8589934592 | bytes 8388608 | tf_op jit(solution)/shard_map/pallas_call | solution.py:381
  53.9 2.7 %shard_map.131 = (f32[32,512]{1,0:T(8,128)}, f32[1,1]{1,0:T(1,128)}, f32[1,1]{1,0:T(1,128)}) custom-call(f32[32,512]{1,0:T(8,128)} %get-tuple-element.9.refs_0_, f32[1,1]{1,0:T(1,128)} %get-tuple-element.10.refs_1_, f32[1,1]{1,0:T(1,128)} %get-tuple-element.11.refs_2_), custom_call_target="tpu_custom_call" | custom-call | tf_op jit(solution)/shard_map/pallas_call | solution.py:393
